TPU v7x, 256 devices: a whole 4x4x8 slice. The times are simulated.
256 devices in a mesh: grp: 8 (over y, core), path: 32 (over x, z).
Axes of the slice: x: 4, y: 4, z: 8, core: 2. Of those that a mesh axis runs over, the one named last changes fastest.
Arguments:
- start_rates: float32 [256, 80], P('grp'), may hold values from 1 to 6
- loadings: float32 [256, 80, 80], P('grp'), may hold values from -0.15625 to 0.15625
- stress: float32 [80], replicated, may hold values from 0.5 to 1.5
- increments: bfloat16 [256, 2, 80, 8192], P('grp', None, None, 'path'), may hold values from -6 to 6
- cotangent: float32 [256, 80, 8192], P('grp', None, 'path'), may hold values from 0.5 to 1.5
- first_active: int32 [256], P('grp'), may hold values from 0 to 39
Outputs:
- rate_adjoint: float32 [256, 80], P(('grp', 'path'))
- vol_gradient: float32 [256, 80, 80], P(('grp', 'path'))
- stress_gradient: float32 [80], replicated
Inputs may be any that keep to these rules, and one draw needn't show every extreme that they name: `first_active`: rates below a scenario's first active index have expired and stay fixed.
All inputs are finite; a program needn't handle non-finite values.
Results may differ from a plain program's by a relative error of at most 0.0003.
Values sent between devices are 32-bit elements; how exact they have to be, the bound alone decides.
A program may use at most 64 MiB of HBM per device.

v0:
```python
import jax
import jax.numpy as jnp
from jax import lax
from jax.sharding import PartitionSpec as P

RATE_SCALE = 0.01


def advance(rates, lam, active, shocks):
    highest = lax.Precision.HIGHEST
    cov = jnp.einsum("sif,sjf->sij", lam, lam, precision=highest)
    count = lam.shape[1]
    lower = (jnp.arange(count)[:, None] >= jnp.arange(count)[None, :]).astype(jnp.float32)
    accrual = active * (RATE_SCALE * rates / (1.0 + RATE_SCALE * rates))
    drift = jnp.einsum("sij,sjp->sip", cov * lower[None], accrual, precision=highest)
    half_var = 0.5 * jnp.diagonal(cov, axis1=1, axis2=2)[:, :, None]
    shock = jnp.einsum("sif,sfp->sip", lam, shocks, precision=highest)
    return rates * jnp.exp(active * (drift - half_var + shock))


def body(start_rates, loadings, stress, increments, cotangent, first_active):
    total_paths = cotangent.shape[2] * lax.axis_size("path")
    rate_index = jnp.arange(loadings.shape[1])
    active = (rate_index[None, :] >= first_active[:, None]).astype(jnp.float32)[:, :, None]
    lam = stress[None, :, None] * loadings
    early = increments[:, 0].astype(jnp.float32)
    late = increments[:, 1].astype(jnp.float32)
    scaled = cotangent / total_paths
    shape_full = cotangent.shape

    def first_step(rates0, lam_in):
        return advance(jnp.broadcast_to(rates0[:, :, None], shape_full), lam_in, active, early)

    def second_step(rates1, lam_in):
        return advance(rates1, lam_in, active, late)

    mid, back_first = jax.vjp(first_step, start_rates, lam)
    final, back_second = jax.vjp(second_step, mid, lam)
    bar_mid, bar_late = back_second(scaled)
    summed_late = lax.psum_scatter(bar_late, "path", scatter_dimension=0, tiled=True)
    bar_start, bar_early = back_first(bar_mid)
    summed_early, rate_adjoint = (
        lax.psum_scatter(bar_early, "path", scatter_dimension=0, tiled=True),
        lax.psum_scatter(bar_start, "path", scatter_dimension=0, tiled=True),
    )
    bar_lam = summed_late + summed_early
    owned = bar_lam.shape[0]
    offset = lax.axis_index("path") * owned
    mine = lax.dynamic_slice_in_dim(loadings, offset, owned, 0)
    stress_gradient = lax.psum(jnp.sum(mine * bar_lam, axis=(0, 2)), ("grp", "path"))
    vol_gradient = stress[None, :, None] * bar_lam
    return (rate_adjoint, vol_gradient, stress_gradient)


def solution(mesh):
    return jax.shard_map(
        body,
        mesh=mesh,
        in_specs=(
            P("grp", None),
            P("grp", None, None),
            P(),
            P("grp", None, None, "path"),
            P("grp", None, "path"),
            P("grp"),
        ),
        out_specs=(P(("grp", "path"), None), P(("grp", "path"), None, None), P()),
        check_vma=False,
    )
```

profile of v0, /device:TPU:1, one launch (start us, length us, event | category | flops | bytes accessed | tf_op | source)
XLA Modules:
  0.0 396.2 jit_solution(589833978775759352)
XLA Ops:
  8.8 4.2 %fusion.34 = f32[32,80,80]{2,1,0:T(8,128)S(1)} fusion(f32[32,80,80]{2,1,0:T(8,128)} %param.7, f32[80]{0:T(128)} %param.8), kind=kOutput, calls=%fused_computation.51 | convolution fusion | flops 196812800 | bytes 1638720 | tf_op jit(solution)/shard_map/jvp(sif,sjf->sij)/dot_general | solution.py:11
  13.0 2.8 copy.21
  15.8 3.4 gather_fusion
  24.0 3.3 fusion.25
  27.4 3.2 fusion.61
  30.5 2.7 fusion.10
  33.3 4.3 %convolution_multiply_fusion.1 = f32[32,80,80]{2,1,0:T(8,128)} fusion(f32[32,80,256]{2,1,0:T(8,128)S(1)} %get-tuple-element.4, f32[80,80]{1,0:T(8,128)S(1)} %fusion.49, f32[32,80,256]{2,1,0:T(8,128)S(1)} %multiply_exponential_fusion.1, f32[32,80]{1,0:T(8,128)S(1)} %copy-done.8, f32[32,80]{1,0:T(8,128)S(1)} %fusion.50), kind=kOutput, calls=%fused_computation.26 | convolution fusion | flops 632627200 | bytes 6108160 | tf_op jit(solution)/shard_map/transpose(jvp(sij,sjp->sip))/dot_general | solution.py:15
  37.6 5.5 %fusion.60 = (f32[32,80]{1,0:T(8,128)S(1)}, f32[32,80,256]{2,1,0:T(8,128)S(1)}) fusion(f32[32,80,256]{2,1,0:T(8,128)S(1)} %multiply_exponential_fusion.1, f32[32,80]{1,0:T(8,128)S(1)} %copy-done.8, f32[32,80]{1,0:T(8,128)S(1)} %fusion.50, f32[32,80,256]{2,1,0:T(8,128)S(1)} %get-tuple-element.4, f32[32,80,80]{2,1,0:T(8,128)S(1)} %fusion.34, ...), kind=kOutput, calls=%fused_computation.89 | convolution fusion | flops 642455040 | bytes 13982720 | tf_op jit(solution)/shard_map/transpose(jvp(sij,sjp->sip))/dot_general | solution.py:15
  43.1 2.8 fusion.13
  45.8 4.0 %convolution_multiply_fusion = f32[32,80,80]{2,1,0:T(8,128)} fusion(f32[32,80]{1,0:T(8,128)S(1)} %get-tuple-element.9, f32[80,80]{1,0:T(8,128)S(1)} %fusion.49, f32[32,80,256]{2,1,0:T(8,128)S(1)} %multiply_exponential_fusion.1, f32[32,80,256]{2,1,0:T(8,128)S(1)} %get-tuple-element.13, f32[32,80]{1,0:T(8,128)S(1)} %copy-done.8, f32[32,80]{1,0:T(8,128)S(1)} %fusion.50), kind=kOutput, calls=%fused_computation.25 | convolution fusion | flops 631316480 | bytes 6118400 | tf_op jit(solution)/shard_map/transpose(jvp(sij,sjp->sip))/dot_general | solution.py:15
  49.8 3.3 copy.27
  53.2 8.5 %scatter_fusion = f32[32,80,80]{0,2,1:T(8,128)} fusion(f32[32,80,80]{0,2,1:T(8,128)} %copy.27, s32[80]{0:T(128)S(1)} %fusion.54, f32[80,32]{1,0:T(8,128)S(1)} %copy.28), kind=kCustom, calls=%fused_computation.1 | custom fusion | flops 2560 | bytes 31360 | tf_op jit(solution)/shard_map/transpose(jvp(jit(diagonal)))/scatter-add | solution.py:16
  61.7 3.5 copy.30
  65.2 4.1 %convolution_add_fusion.3 = f32[32,80,80]{2,1,0:T(8,128)S(1)} fusion(f32[32,80,80]{2,1,0:T(8,128)} %fusion.10, f32[32,80,80]{2,1,0:T(8,128)} %copy.30, f32[32,80,80]{2,1,0:T(8,128)S(1)} %copy-done, f32[80]{0:T(128)S(1)} %copy-done.9), kind=kOutput, calls=%fused_computation.24 | convolution fusion | flops 197017600 | bytes 3277120 | tf_op jit(solution)/shard_map/transpose(jvp(sif,sjf->sij))/dot_general | solution.py:11
  69.3 2.6 convolution_add_fusion.2
  71.9 3.3 copy.31
  75.3 8.5 %scatter_fusion.1 = f32[32,80,80]{0,2,1:T(8,128)} fusion(f32[32,80,80]{0,2,1:T(8,128)} %copy.31, s32[80]{0:T(128)S(1)} %fusion.54, f32[80,32]{1,0:T(8,128)S(1)} %copy.32), kind=kCustom, calls=%fused_computation.2 | custom fusion | flops 2560 | bytes 31360 | tf_op jit(solution)/shard_map/transpose(jvp(jit(diagonal)))/scatter-add | solution.py:16
  83.8 3.3 copy.34
  87.1 4.1 %convolution_add_fusion.1 = f32[32,80,80]{2,1,0:T(8,128)S(1)} fusion(f32[32,80,80]{2,1,0:T(8,128)} %fusion.13, f32[32,80,80]{2,1,0:T(8,128)} %copy.34, f32[32,80,80]{2,1,0:T(8,128)S(1)} %copy-done, f32[80]{0:T(128)S(1)} %copy-done.9), kind=kOutput, calls=%fused_computation.22 | convolution fusion | flops 197017600 | bytes 3277120 | tf_op jit(solution)/shard_map/transpose(jvp(sif,sjf->sij))/dot_general | solution.py:11
  91.3 2.7 fusion.9
  94.6 9.8 %add_reduce_fusion = f32[32,80]{1,0:T(8,128)S(1)} fusion(f32[32,80,256]{2,1,0:T(8,128)} %copy-done.5, f32[32,80,256]{2,1,0:T(8,128)} %copy-done.1, f32[32,80]{1,0:T(8,128)S(1)} %get-tuple-element.8, f32[32,80]{1,0:T(8,128)S(1)} %get-tuple-element.10, f32[32,80]{1,0:T(8,128)S(1)} %get-tuple-element.7, f32[32,80]{1,0:T(8,128)S(1)} %fusion.50, ...), kind=kOutput, calls=%fused_computation.15 | convolution fusion | flops 638522880 | bytes 6149120 | tf_op jit(solution)/shard_map/transpose(jvp(sij,sjp->sip))/dot_general | solution.py:15
  104.4 118.7 %all-reduce = f32[32,80]{1,0:T(8,128)S(1)} all-reduce(f32[32,80]{1,0:T(8,128)S(1)} %add_reduce_fusion), channel_id=3, replica_groups=mesh['grp'=8,'path'=32] {'path'}, use_global_device_ids=true, to_apply=%region_1.2.clone | all-reduce | flops 2560 | bytes 20480
  224.3 83.4 %reduce-scatter.2.cloned.1.call-done = f32[1,80,80]{2,1,0:T(8,128)} async-done(((f32[32,80,80]{2,1,0:T(8,128)}), f32[1,80,80]{2,1,0:T(8,128)}) %reduce-scatter.2.cloned.1.call-update) | async-done | bytes 25616 | tf_op jit(solution)/shard_map/reduce_scatter | solution.py:40
  309.2 79.8 %psum.7 = f32[80]{0:T(128)} all-reduce(f32[80]{0:T(128)S(1)} %get-tuple-element.5), channel_id=1, replica_groups=mesh['grp'=8,'path'=32] {'grp','path'}, use_global_device_ids=true, to_apply=%region_9.10 | all-reduce | flops 80 | bytes 640 | tf_op jit(solution)/shard_map/psum | solution.py:50
  (40 shorter events, 9.8 us)
Async XLA Ops:
  7.2 300.5 %reduce-scatter.2.cloned.1.call-start = ((), (), s32[]{:S(2)}) async-start(), calls=%async_computation.1 | async-start | bytes 1351680 | tf_op jit(solution)/shard_map/reduce_scatter | solution.py:40
  15.8 6.1 %copy-start = (f32[32,80,80]{2,1,0:T(8,128)S(1)}, f32[32,80,80]{2,1,0:T(8,128)}, u32[]{:S(2)}) copy-start(f32[32,80,80]{2,1,0:T(8,128)} %param.7) | copy-start | bytes 2457604
  15.8 6.1 %copy-start.9 = (f32[80]{0:T(128)S(1)}, f32[80]{0:T(128)}, u32[]{:S(2)}) copy-start(f32[80]{0:T(128)} %param.8) | copy-start | bytes 964
  19.4 2.5 copy-start.4
  21.9 2.1 copy-start.8
  24.0 21.8 %copy-start.1 = (f32[32,80,256]{2,1,0:T(8,128)}, f32[32,80,256]{2,1,0:T(8,128)S(1)}, u32[]{:S(2)}) copy-start(f32[32,80,256]{2,1,0:T(8,128)S(1)} %multiply_exponential_fusion.1) | copy-start | bytes 7864324
  24.0 3.4 copy-start.7
  43.1 2.8 copy-start.5
  65.2 4.1 %copy-start.3 = (f32[32,80,80]{2,1,0:T(8,128)S(1)}, f32[32,80,80]{2,1,0:T(8,128)}, u32[]{:S(2)}) copy-start(f32[32,80,80]{2,1,0:T(8,128)} %copy.30) | copy-start | bytes 2457604
  87.1 4.2 %copy-start.2 = (f32[32,80,80]{2,1,0:T(8,128)S(1)}, f32[32,80,80]{2,1,0:T(8,128)}, u32[]{:S(2)}) copy-start(f32[32,80,80]{2,1,0:T(8,128)} %copy.34) | copy-start | bytes 2457604
  87.1 4.2 %copy-start.6 = (f32[32,80,80]{2,1,0:T(8,128)S(1)}, f32[32,80,80]{2,1,0:T(8,128)}, u32[]{:S(2)}) copy-start(f32[32,80,80]{2,1,0:T(8,128)} %convolution_add_fusion.2) | copy-start | bytes 2457604
  91.3 2.7 copy-start.10
Sparse Core Ops, SparseCore 0:
  94.2 213.4 reduce-scatter.1
where the time goes:
time: 400 us; the launch traced here: 396 us
  blocking collectives  199 us (50%)
  waiting for transfers between devices  83.4 us (21%)
  matrix products  57.8 us (14%)
  local copies, waits for them, and re-layouts  21.6 us (5%)
  other arithmetic  20.2 us (5%)
  between operations  14.5 us (4%)
    unnamed x1, blocking collectives  119 us
    reduce_scatter x1, waiting for transfers between devices, body(): lax.psum_scatter(bar_late, 'path', scatter_dimension=0, tiled=True)  83.4 us
    psum x1, blocking collectives, body(): lax.psum(jnp.sum(mine * bar_lam, axis=(0, 2)), ('grp', 'path'))  79.8 us
    dot_general x6, matrix products, advance(): jnp.einsum('sij,sjp->sip', cov * lower[None], accrual, precision=highest)  29.4 us
    dot_general x5, matrix products, advance(): cov = jnp.einsum('sif,sjf->sij', lam, lam, precision=highest)  17.8 us
    scatter-add x2, other arithmetic, advance(): half_var = 0.5 * jnp.diagonal(cov, axis1=1, axis2=2)[:, :, None]  17 us
    dot_general x4, matrix products, advance(): shock = jnp.einsum('sif,sfp->sip', lam, shocks, precision=highest)  10.7 us
  transfers between devices with their start and end apart: 1, of which 1 were waited for; matrix products, arithmetic and copies ran while one was open for 3% of the time, Pallas kernels for 0%

commit v1 on v0

v1 whole, which is shorter than its diff:
```python
import math

import jax
import jax.numpy as jnp
from jax import lax
from jax.experimental import pallas as pl
from jax.experimental.pallas import tpu as pltpu
from jax.sharding import PartitionSpec as P

NR = 80
WIDTH = 256
X, Z, G = 4, 8, 8
PAIRS = 16
PACKED = 56
LN2 = math.log(2.0)
LOG2E = 1.0 / LN2
bf16 = jnp.bfloat16
f32 = jnp.float32
MESH = pl.DeviceIdType.MESH


def dot(a, b):
    return jnp.dot(a, b, preferred_element_type=f32)


def dot_nt(a, b):
    return lax.dot_general(a, b, (((1,), (1,)), ((), ())), preferred_element_type=f32)


def split(value):
    high = value.astype(bf16)
    return high, (value - high.astype(f32)).astype(bf16)


def index_masks():
    rows = lax.broadcasted_iota(jnp.int32, (NR, NR), 0)
    cols = lax.broadcasted_iota(jnp.int32, (NR, NR), 1)
    return rows, cols


def pair_place(pair, z):
    step, way = pair // 2, pair % 2
    reach = 4 - (step + 1) // 2
    target = lax.rem(z + reach * (1 - way) + (Z - reach) * way, Z)
    return target, lax.rem(step + way, 2)


def scaled_loadings(load, stress_col, first, rows):
    return jnp.where(rows >= first, load * stress_col, 0.0) * LOG2E


def adjoint_of(items, stress_col, log_paths, emit):
    rows, cols = index_masks()
    low, upp, eye = rows >= cols, rows <= cols, rows == cols
    ones = jnp.ones((16, WIDTH), bf16)
    gap = jnp.zeros((32, WIDTH), bf16)
    for d in items:
        d["lam"] = scaled_loadings(d["load"][...], stress_col, d["first"], rows)
        d["lh"], d["ll"] = split(d["lam"])
    for d in items:
        d["cov"] = dot_nt(d["lh"], d["lh"])
    for d in items:
        drift = jnp.where(low, d["cov"], 0.0) * LN2
        r0 = d["r0"]
        d["a0"] = r0 / (100.0 + r0)
        half = jnp.sum(d["lam"] * d["lam"], axis=1, keepdims=True) * (-0.5 * LN2)
        d["c1"] = half + jnp.sum(drift * d["a0"] + jnp.where(eye, jnp.log2(r0), 0.0), axis=1, keepdims=True)
        d["c2"] = half - log_paths
        d["left"] = jnp.concatenate([d["lh"], d["ll"], drift.astype(bf16)], axis=1)
        d["back"] = (jnp.where(upp, d["cov"], 0.0) * (LN2 * LN2)).astype(bf16)
    for d in items:
        z1 = d["z"][0]
        d["e1"] = dot(d["left"][:, : 2 * NR], jnp.concatenate([z1, z1], axis=0))
    for d in items:
        mid = jnp.exp2(d["e1"] + d["c1"])
        scaled = 0.01 * mid
        inverse = 1.0 / (1.0 + scaled)
        accrual = scaled * inverse
        d["mid"], d["a"], d["slope"] = mid, accrual.astype(bf16), accrual * inverse
    for d in items:
        z2 = d["z"][1]
        d["e2"] = dot(d["left"], jnp.concatenate([z2, z2, d["a"]], axis=0))
    for d in items:
        d["g2"] = d["mid"] * jnp.exp2(d["e2"] + d["c2"]) * d["cot"][...]
        d["g2h"], d["g2l"] = split(d["g2"])
    for d in items:
        d["da"] = dot(d["back"], d["g2h"])
    for d in items:
        right = jnp.concatenate([d["z"][1], ones, gap, d["a"]], axis=0)
        d["sums2"] = dot_nt(jnp.concatenate([d["g2h"], d["g2l"]], axis=0), right)
    for d in items:
        g1h, g1l = split(d["g2"] + d["slope"] * d["da"])
        right = jnp.concatenate([d["z"][0], ones], axis=0)
        d["sums1"] = dot_nt(jnp.concatenate([g1h, g1l], axis=0), right)
    for d in items:
        sum1 = d["sums1"][:NR] + d["sums1"][NR:]
        sum2 = d["sums2"][:NR, :128] + d["sums2"][NR:, :128]
        outer = d["sums2"][:NR, 128:208] + d["sums2"][NR:, 128:208]
        total1, total2 = sum1[:, NR : NR + 1], sum2[:, NR : NR + 1]
        bar_cov = jnp.where(low, outer + total1 * d["a0"], 0.0)
        mh, ml = split((bar_cov + bar_cov.T) * LN2)
        through = dot(
            jnp.concatenate([mh, ml, mh], axis=1), jnp.concatenate([d["lh"], d["lh"], d["ll"]], axis=0)
        )
        bar = sum1[:, :NR] + sum2[:, :NR] + through - ((total1 + total2) * LN2) * d["lam"]
        emit(d, jnp.where(rows >= d["first"], bar, 0.0), total1)


def pack(ref, bar, total):
    ref[:, 0:NR] = bar[:PACKED]
    ref[:, NR : NR + 1] = total[:PACKED]
    rest = jnp.concatenate([bar[PACKED:], total[PACKED:]], axis=1)
    ref[0:24, 81:128] = rest[:, 0:47]
    ref[24:48, 81:115] = rest[:, 47:81]
    ref[24:48, 115:128] = jnp.zeros((24, 13), f32)
    ref[48:56, 81:128] = jnp.zeros((8, 47), f32)


def unpack(value):
    rest = jnp.concatenate([value[0:24, 81:128], value[24:48, 81:115]], axis=1)
    bar = jnp.concatenate([value[:, 0:NR], rest[:, 0:NR]], axis=0)
    total = jnp.concatenate([value[:, NR : NR + 1], rest[:, NR : NR + 1]], axis=0)
    return bar, total


def kernel(
    log_paths,
    stress_ref, first_ref, start_ref, load_hbm, z_hbm, cot_hbm,
    rate_out, vol_out, stress_out,
    load_v, z_v, cot_v, out_buf, ring_buf, x_buf, acc, sx, sz, sg,
    in_sem, ring_send, ring_recv, x_send, x_recv, s_send, s_recv,
):
    g = lax.axis_index("grp")
    path = lax.axis_index("path")
    x, z = path // Z, lax.rem(path, Z)

    def fetches(pair):
        target, half = pair_place(pair, z)
        blocks = pl.ds(2 * half, 2)
        return [
            pltpu.make_async_copy(hbm.at[blocks, target], vmem.at[pair], in_sem.at[i, pair])
            for i, (hbm, vmem) in enumerate(((load_hbm, load_v), (z_hbm, z_v), (cot_hbm, cot_v)))
        ]

    @pl.loop(0, PAIRS)
    def _(pair):
        for copy in fetches(pair):
            copy.start()

    def x_peer(k):
        return (g, lax.rem(x + k, X) * Z + z)

    def z_peer(k):
        return (g, x * Z + lax.rem(z + k, Z))

    def g_peer(k):
        return (lax.rem(g + k, G), path)

    barrier = pltpu.get_barrier_semaphore()
    peers = [(x_peer, X), (z_peer, Z), (g_peer, G)]
    for peer, size in peers:
        for k in range(1, size):
            pl.semaphore_signal(barrier, inc=1, device_id=peer(k), device_id_type=MESH)

    rows, cols = index_masks()
    eye = rows == cols
    stress_col = jnp.sum(jnp.where(eye, stress_ref[...], 0.0), axis=1, keepdims=True)
    acc[...] = jnp.zeros_like(acc)

    def ring(way, step):
        return pltpu.make_async_remote_copy(
            src_ref=out_buf.at[2 * step + way],
            dst_ref=ring_buf.at[way, step],
            send_sem=ring_send.at[way, step],
            recv_sem=ring_recv.at[way, step],
            device_id=z_peer(Z - 1 if way else 1),
            device_id_type=MESH,
        )

    def emit(d, bar, total):
        pack(d["out"], bar, total)
        acc[...] += d["load"][...] * bar

    def scenario(pair, k):
        target, half = pair_place(pair, z)
        s = (2 * half + k) * Z + target
        return dict(
            load=load_v.at[pair, k], z=z_v.at[pair, k], cot=cot_v.at[pair, k], out=out_buf.at[pair, k],
            first=first_ref[s], r0=start_ref[pl.ds(s, 1), :],
        )

    @pl.loop(0, 4)
    def _(group):
        for j in range(4):
            for copy in fetches(4 * group + j):
                copy.wait()
        items = [scenario(4 * group + j, k) for j in range(4) for k in range(2)]
        adjoint_of(items, stress_col, log_paths, emit)

        @pl.when(group == 0)
        def _():
            pl.semaphore_wait(barrier, X + Z + G - 3)

        for j in range(2):
            step = 2 * group + j
            for way in range(2):

                @pl.when(group > 0)
                def _():
                    ring(way, step - 2).wait_recv()
                    out_buf[2 * step + way] += ring_buf[way, step - 2]

                @pl.when(step < 7)
                def _():
                    ring(way, step).start()

    def share(stage, buf, peer, size, me, base):
        return [
            pltpu.make_async_remote_copy(
                src_ref=buf.at[me],
                dst_ref=buf.at[me],
                send_sem=s_send.at[base + k],
                recv_sem=s_recv.at[base + k],
                device_id=peer(k),
                device_id_type=MESH,
            )
            for k in range(1, size)
        ]

    def summed(buf, size):
        total = buf[0]
        for i in range(1, size):
            total = total + buf[i]
        return total

    stress_part = jnp.sum(jnp.where(eye, jnp.sum(acc[...], axis=1, keepdims=True), 0.0), axis=0, keepdims=True)
    sx[x, :, 0:NR] = jnp.broadcast_to(stress_part, (8, NR))
    sx[x, :, NR:128] = jnp.zeros((8, 128 - NR), f32)
    stage_x = share(0, sx, x_peer, X, x, 0)
    for copy in stage_x:
        copy.start()

    for copy in stage_x:
        copy.wait_recv()
    sz[z] = summed(sx, X)
    stage_z = share(1, sz, z_peer, Z, z, X)
    for copy in stage_z:
        copy.start()

    for way in range(2):
        ring(way, 6).wait_recv()
        out_buf[15 - way] += ring_buf[way, 6]

    def mine(at):
        return out_buf.at[15 - at // 2, lax.rem(at, 2)]

    stage_out = [
        pltpu.make_async_remote_copy(
            src_ref=mine(lax.rem(x + k, X)),
            dst_ref=x_buf.at[k - 1],
            send_sem=x_send.at[k - 1],
            recv_sem=x_recv.at[k - 1],
            device_id=x_peer(k),
            device_id_type=MESH,
        )
        for k in range(1, X)
    ]
    for copy in stage_out:
        copy.start()

    for copy in stage_z:
        copy.wait_recv()
    sg[g] = summed(sz, Z)
    stage_g = share(2, sg, g_peer, G, g, X + Z)
    for copy in stage_g:
        copy.start()

    lam = scaled_loadings(load_v[15 - x // 2, lax.rem(x, 2)], stress_col, first_ref[path], rows)
    lh, ll = split(lam)
    cov = (dot_nt(lh, lh) + dot_nt(lh, ll) + dot_nt(ll, lh)) * (LN2 * LN2)
    r0 = start_ref[pl.ds(path, 1), :]

    for copy in stage_out:
        copy.wait_recv()
    bar, total = unpack(mine(x)[...] + x_buf[0] + x_buf[1] + x_buf[2])
    vol_out[0] = stress_col * bar
    through = jnp.sum(jnp.where(rows >= cols, cov, 0.0) * total, axis=0, keepdims=True)
    direct = jnp.sum(jnp.where(eye, total, 0.0), axis=0, keepdims=True)
    rate_out[...] = direct / r0 + through * (100.0 / ((100.0 + r0) * (100.0 + r0)))

    for copy in stage_g:
        copy.wait_recv()
    stress_out[...] = summed(sg, G)[0:1, 0:NR]

    @pl.loop(0, 7)
    def _(step):
        for way in range(2):
            ring(way, step).wait_send()

    for copy in stage_x + stage_z + stage_g + stage_out:
        copy.wait_send()


def body(start_rates, loadings, stress, increments, cotangent, first_active):
    log_paths = math.log2(WIDTH * X * Z)
    vmem = pl.BlockSpec(memory_space=pltpu.VMEM)
    smem = pl.BlockSpec(memory_space=pltpu.SMEM)
    anywhere = pl.BlockSpec(memory_space=pl.ANY)
    dma = pltpu.SemaphoreType.DMA
    rate, vol, stress_gradient = pl.pallas_call(
        lambda *refs: kernel(log_paths, *refs),
        out_shape=(
            jax.ShapeDtypeStruct((1, NR), f32),
            jax.ShapeDtypeStruct((1, NR, NR), f32),
            jax.ShapeDtypeStruct((1, NR), f32),
        ),
        in_specs=[vmem, smem, vmem, anywhere, anywhere, anywhere],
        out_specs=(vmem, vmem, vmem),
        scratch_shapes=[
            pltpu.VMEM((PAIRS, 2, NR, NR), f32),
            pltpu.VMEM((PAIRS, 2, 2, NR, WIDTH), bf16),
            pltpu.VMEM((PAIRS, 2, NR, WIDTH), f32),
            pltpu.VMEM((PAIRS, 2, PACKED, 128), f32),
            pltpu.VMEM((2, 7, 2, PACKED, 128), f32),
            pltpu.VMEM((X - 1, PACKED, 128), f32),
            pltpu.VMEM((NR, NR), f32),
            pltpu.VMEM((X, 8, 128), f32),
            pltpu.VMEM((Z, 8, 128), f32),
            pltpu.VMEM((G, 8, 128), f32),
            dma((3, PAIRS)),
            dma((2, 7)),
            dma((2, 7)),
            dma((X - 1,)),
            dma((X - 1,)),
            dma((X + Z + G,)),
            dma((X + Z + G,)),
        ],
        compiler_params=pltpu.CompilerParams(
            collective_id=0, has_side_effects=True, vmem_limit_bytes=56 * 2**20
        ),
        name="adjoint",
    )(
        stress[None],
        first_active,
        start_rates,
        loadings.reshape(X, Z, NR, NR),
        increments.reshape(X, Z, 2, NR, WIDTH),
        cotangent.reshape(X, Z, NR, WIDTH),
    )
    return rate, vol, stress_gradient[0]


def solution(mesh):
    return jax.shard_map(
        body,
        mesh=mesh,
        in_specs=(
            P("grp", None),
            P("grp", None, None),
            P(),
            P("grp", None, None, "path"),
            P("grp", None, "path"),
            P("grp"),
        ),
        out_specs=(P(("grp", "path"), None), P(("grp", "path"), None, None), P()),
        check_vma=False,
    )
```

time: 400 us -> 42.5 us (0.11)
  blocking collectives: 199 us -> 0 us
  waiting for transfers between devices: 83.4 us -> 0 us
  matrix products: 57.8 us -> 0 us
  Pallas kernels: 0 us -> 38 us
  other arithmetic: 20.2 us -> 0 us
  local copies, waits for them, and re-layouts: 21.6 us -> 3.66 us
  between operations: 14.5 us -> 0.64 us
    unnamed x1 -> x0, blocking collectives: 119 us -> none
    reduce_scatter x1 -> x0, waiting for transfers between devices: 83.4 us -> none  [body(): lax.psum_scatter(bar_late, 'path', scatter_dimension=0, tiled=True)]
    psum x1 -> x0, blocking collectives: 79.8 us -> none  [body(): lax.psum(jnp.sum(mine * bar_lam, axis=(0, 2)), ('grp', 'path'))]
    dot_general x15 -> x0, matrix products: 57.8 us -> none  [the longest x6 29.4 us: advance(): jnp.einsum('sij,sjp->sip', cov * lower[None], accrual, precision=highest)]
    pallas_call x0 -> x1, Pallas kernels: none -> 38 us  [body(): pl.pallas_call(lambda *refs: kernel(log_paths, *refs), out_shape=(jax.Sha...]
    scatter-add x2 -> x0, other arithmetic: 17 us -> none  [advance(): half_var = 0.5 * jnp.diagonal(cov, axis1=1, axis2=2)[:, :, None]]
    mul x5 -> x0, local copies, waits for them, and re-layouts: 6.83 us -> none  [the longest x2 6.59 us: advance(): cov * lower[None]]
    scatter-add x2 -> x0, local copies, waits for them, and re-layouts: 6.77 us -> none  [advance(): half_var = 0.5 * jnp.diagonal(cov, axis1=1, axis2=2)[:, :, None]]
  transfers between devices with their start and end apart: 1 -> 0, of which waited for: 1 -> 0; matrix products, arithmetic and copies ran while one was open for 3% -> 0% of each run, Pallas kernels for 0% -> 0%
where the time goes in v1:
time: 42.5 us; the launch traced here: 42.3 us
  Pallas kernels  38 us (89%)
  local copies, waits for them, and re-layouts  3.66 us (9%)
  between operations  0.64 us (2%)
    pallas_call x1, Pallas kernels, body(): pl.pallas_call(lambda *refs: kernel(log_paths, *refs), out_shape=(jax.Sha...  38 us
    unnamed x3, local copies, waits for them, and re-layouts  3.66 us

profile of v1, /device:TPU:1, one launch (start us, length us, event | category | flops | bytes accessed | tf_op | source)
XLA Modules:
  0.0 42.3 jit_solution(1908404056002943192)
XLA Ops:
  0.6 38.0 %adjoint.1 = (f32[1,80]{1,0:T(1,128)}, f32[1,80,80]{2,1,0:T(8,128)}, f32[1,80]{1,0:T(1,128)}) custom-call(f32[1,80]{1,0:T(1,128)} %bitcast.8, s32[32]{0:T(128)} %refs_1_.1, f32[32,80]{1,0:T(8,128)} %refs_2_.1, f32[4,8,80,80]{3,2,1,0:T(8,128)} %bitcast.7, bf16[4,8,2,80,256]{4,3,2,1,0:T(8,128)(2,1)} %bitcast.5, f32[4,8,80,256]{3,2,1,0:T(8,128)} %bitcast.6), custom_call_target="tpu_custom_call" | custom-call | tf_op jit(solution)/shard_map/adjoint/pallas_call | solution.py:310
  38.6 1.1 %copy.12 = f32[1,80]{1,0:T(1,128)} copy(f32[1,80]{1,0:T(1,128)} %get-tuple-element.12) | data formatting | bytes 640
  39.8 1.4 %copy.13 = f32[1,80,80]{2,1,0:T(8,128)} copy(f32[1,80,80]{2,1,0:T(8,128)} %get-tuple-element.13) | data formatting | bytes 51200
  41.2 1.1 %copy.14 = f32[80]{0:T(128)} copy(f32[80]{0:T(128)} %bitcast.9) | data formatting | bytes 640

commit v2 on v1

v2 whole, which is shorter than its diff:
```python
import math

import jax
import jax.numpy as jnp
from jax import lax
from jax.experimental import pallas as pl
from jax.experimental.pallas import tpu as pltpu
from jax.sharding import PartitionSpec as P

NR = 80
WIDTH = 256
X, Z = 4, 8
Y, CORES = 4, 2
SIXTEEN = X * Y
PAIRS = 16
PACKED = 56
LN2 = math.log(2.0)
LOG2E = 1.0 / LN2
bf16 = jnp.bfloat16
f32 = jnp.float32
MESH = pl.DeviceIdType.MESH


def dot(a, b):
    return jnp.dot(a, b, preferred_element_type=f32)


def dot_nt(a, b):
    return lax.dot_general(a, b, (((1,), (1,)), ((), ())), preferred_element_type=f32)


def split(value):
    high = value.astype(bf16)
    return high, (value - high.astype(f32)).astype(bf16)


def index_masks():
    rows = lax.broadcasted_iota(jnp.int32, (NR, NR), 0)
    cols = lax.broadcasted_iota(jnp.int32, (NR, NR), 1)
    return rows, cols


def place(pair, k, x, z):
    half, step, way = pair // 8, pair % 8 // 2, pair % 2
    reach = 2 - (step + 1) // 2
    side = lax.rem(step + way, 2)
    hops = 3 - 2 * half - side if k else 4 + 2 * half + side
    return lax.rem(x + reach * (1 - way) + (X - reach) * way, X), hops


def scaled_loadings(load, stress_col, first, rows):
    return jnp.where(rows >= first, load * stress_col, 0.0) * LOG2E


def adjoint_of(items, stress_col, log_paths, emit):
    rows, cols = index_masks()
    low, upp, eye = rows >= cols, rows <= cols, rows == cols
    ones = jnp.ones((16, WIDTH), bf16)
    gap = jnp.zeros((32, WIDTH), bf16)
    for d in items:
        d["lam"] = scaled_loadings(d["load"][...], stress_col, d["first"], rows)
        d["lh"], d["ll"] = split(d["lam"])
    for d in items:
        d["cov"] = dot_nt(d["lh"], d["lh"])
    for d in items:
        drift = jnp.where(low, d["cov"], 0.0) * LN2
        r0 = d["r0"]
        d["a0"] = r0 / (100.0 + r0)
        half = jnp.sum(d["lam"] * d["lam"], axis=1, keepdims=True) * (-0.5 * LN2)
        d["c1"] = half + jnp.sum(drift * d["a0"] + jnp.where(eye, jnp.log2(r0), 0.0), axis=1, keepdims=True)
        d["c2"] = half - log_paths
        d["left"] = jnp.concatenate([d["lh"], d["ll"], drift.astype(bf16)], axis=1)
        d["back"] = (jnp.where(upp, d["cov"], 0.0) * (LN2 * LN2)).astype(bf16)
    for d in items:
        z1 = d["z"][0]
        d["e1"] = dot(d["left"][:, : 2 * NR], jnp.concatenate([z1, z1], axis=0))
    for d in items:
        mid = jnp.exp2(d["e1"] + d["c1"])
        scaled = 0.01 * mid
        inverse = 1.0 / (1.0 + scaled)
        accrual = scaled * inverse
        d["mid"], d["a"], d["slope"] = mid, accrual.astype(bf16), accrual * inverse
    for d in items:
        z2 = d["z"][1]
        d["e2"] = dot(d["left"], jnp.concatenate([z2, z2, d["a"]], axis=0))
    for d in items:
        d["g2"] = d["mid"] * jnp.exp2(d["e2"] + d["c2"]) * d["cot"][...]
        d["g2h"], d["g2l"] = split(d["g2"])
    for d in items:
        d["da"] = dot(d["back"], d["g2h"])
    for d in items:
        right = jnp.concatenate([d["z"][1], ones, gap, d["a"]], axis=0)
        d["sums2"] = dot_nt(jnp.concatenate([d["g2h"], d["g2l"]], axis=0), right)
    for d in items:
        g1h, g1l = split(d["g2"] + d["slope"] * d["da"])
        right = jnp.concatenate([d["z"][0], ones], axis=0)
        d["sums1"] = dot_nt(jnp.concatenate([g1h, g1l], axis=0), right)
    for d in items:
        sum1 = d["sums1"][:NR] + d["sums1"][NR:]
        sum2 = d["sums2"][:NR, :128] + d["sums2"][NR:, :128]
        outer = d["sums2"][:NR, 128:208] + d["sums2"][NR:, 128:208]
        total1, total2 = sum1[:, NR : NR + 1], sum2[:, NR : NR + 1]
        bar_cov = jnp.where(low, outer + total1 * d["a0"], 0.0)
        mh, ml = split((bar_cov + bar_cov.T) * LN2)
        through = dot(
            jnp.concatenate([mh, ml, mh], axis=1), jnp.concatenate([d["lh"], d["lh"], d["ll"]], axis=0)
        )
        bar = sum1[:, :NR] + sum2[:, :NR] + through - ((total1 + total2) * LN2) * d["lam"]
        emit(d, jnp.where(rows >= d["first"], bar, 0.0), total1)


def pack(ref, bar, total):
    ref[:, 0:NR] = bar[:PACKED]
    ref[:, NR : NR + 1] = total[:PACKED]
    rest = jnp.concatenate([bar[PACKED:], total[PACKED:]], axis=1)
    ref[0:24, 81:128] = rest[:, 0:47]
    ref[24:48, 81:115] = rest[:, 47:81]
    ref[24:48, 115:128] = jnp.zeros((24, 13), f32)
    ref[48:56, 81:128] = jnp.zeros((8, 47), f32)


def unpack(value):
    rest = jnp.concatenate([value[0:24, 81:128], value[24:48, 81:115]], axis=1)
    bar = jnp.concatenate([value[:, 0:NR], rest[:, 0:NR]], axis=0)
    total = jnp.concatenate([value[:, NR : NR + 1], rest[:, NR : NR + 1]], axis=0)
    return bar, total


def kernel(
    log_paths,
    stress_hbm, first_hbm, start_hbm, load_hbm, z_hbm, cot_hbm,
    out_hbm,
    stress_ref, first_ref, start_ref, out,
    load_v, z_v, cot_v, out_buf, ring_buf, z_buf, acc, s_plane, s_line,
    small_sem, out_sem, in_sem, ring_send, ring_recv, z_send, z_recv, s_send, s_recv,
):
    g = lax.axis_index("grp")
    path = lax.axis_index("path")
    x, z = path // Z, lax.rem(path, Z)

    def owner(pair, k):
        owner_x, hops = place(pair, k, x, z)
        return owner_x, lax.rem(z + hops, Z)

    def fetches(pair):
        return [
            pltpu.make_async_copy(hbm.at[owner(pair, k)], vmem.at[pair, k], in_sem.at[i, pair, k])
            for k in range(2)
            for i, (hbm, vmem) in enumerate(((load_hbm, load_v), (z_hbm, z_v), (cot_hbm, cot_v)))
        ]

    small = [
        pltpu.make_async_copy(hbm, here, small_sem.at[i])
        for i, (hbm, here) in enumerate(((stress_hbm, stress_ref), (first_hbm, first_ref), (start_hbm, start_ref)))
    ]
    for copy in small:
        copy.start()

    @pl.loop(0, PAIRS)
    def _(pair):
        for copy in fetches(pair):
            copy.start()

    def x_peer(k):
        return (g, lax.rem(x + k, X) * Z + z)

    def z_peer(k):
        return (g, x * Z + lax.rem(z + k, Z))

    y, core = g // CORES, lax.rem(g, CORES)

    def plane_peer(k):
        return (lax.rem(y + k // X, Y) * CORES + core, lax.rem(x + k % X, X) * Z + z)

    def line_peer(k):
        return (y * CORES + lax.rem(core + k // Z, CORES), x * Z + lax.rem(z + k % Z, Z))

    barrier = pltpu.get_barrier_semaphore()
    for k in range(1, SIXTEEN):
        for peer in (plane_peer, line_peer):
            pl.semaphore_signal(barrier, inc=1, device_id=peer(k), device_id_type=MESH)

    for copy in small:
        copy.wait()
    rows, cols = index_masks()
    eye = rows == cols
    stress_col = jnp.sum(jnp.where(eye, stress_ref[...], 0.0), axis=1, keepdims=True)
    acc[...] = jnp.zeros_like(acc)

    def ring(way, half, step):
        return pltpu.make_async_remote_copy(
            src_ref=out_buf.at[8 * half + 2 * step + way],
            dst_ref=ring_buf.at[way, half, step],
            send_sem=ring_send.at[way, half, step],
            recv_sem=ring_recv.at[way, half, step],
            device_id=x_peer(X - 1 if way else 1),
            device_id_type=MESH,
        )

    def hand_over(half, side, k):
        hops = 3 - 2 * half - side if k else 4 + 2 * half + side
        return pltpu.make_async_remote_copy(
            src_ref=out_buf.at[8 * half + 7 - side, k],
            dst_ref=z_buf.at[hops - 1],
            send_sem=z_send.at[hops - 1],
            recv_sem=z_recv.at[hops - 1],
            device_id=z_peer(hops),
            device_id_type=MESH,
        )

    handed = [(0, side, k) for side in range(2) for k in range(2)], [(1, 0, 0), (1, 0, 1), (1, 1, 0)]

    def finish(half):
        for way in range(2):
            ring(way, half, 2).wait_recv()
            out_buf[8 * half + 7 - way] += ring_buf[way, half, 2]
        for what in handed[half]:
            hand_over(*what).start()

    def emit(d, bar, total):
        pack(d["out"], bar, total)
        acc[...] += d["load"][...] * bar

    def scenario(pair, k):
        owner_x, owner_z = owner(pair, k)
        s = owner_x * Z + owner_z
        return dict(
            load=load_v.at[pair, k], z=z_v.at[pair, k], cot=cot_v.at[pair, k], out=out_buf.at[pair, k],
            first=first_ref[s], r0=start_ref[pl.ds(s, 1), :],
        )

    def share(buf, peer, me, stage):
        return [
            pltpu.make_async_remote_copy(
                src_ref=buf.at[me],
                dst_ref=buf.at[me],
                send_sem=s_send.at[stage, k],
                recv_sem=s_recv.at[stage, k],
                device_id=peer(k),
                device_id_type=MESH,
            )
            for k in range(1, SIXTEEN)
        ]

    stage_plane = share(s_plane, plane_peer, y * X + x, 0)
    stage_line = share(s_line, line_peer, core * Z + z, 1)

    @pl.loop(0, 4)
    def _(group):
        for j in range(4):
            for copy in fetches(4 * group + j):
                copy.wait()
        items = [scenario(4 * group + j, k) for j in range(4) for k in range(2)]
        adjoint_of(items, stress_col, log_paths, emit)

        @pl.when(group == 0)
        def _():
            pl.semaphore_wait(barrier, 2 * (SIXTEEN - 1))

        @pl.when(group == 3)
        def _():
            part = jnp.sum(jnp.where(eye, jnp.sum(acc[...], axis=1, keepdims=True), 0.0), axis=0, keepdims=True)
            s_plane[y * X + x, :, 0:NR] = jnp.broadcast_to(part, (8, NR))
            s_plane[y * X + x, :, NR:128] = jnp.zeros((8, 128 - NR), f32)
            for copy in stage_plane:
                copy.start()

        half = group // 2
        for j in range(2):
            step = 2 * (group % 2) + j
            for way in range(2):

                @pl.when(step >= 2)
                def _():
                    ring(way, half, step - 2).wait_recv()
                    out_buf[8 * half + 2 * step + way] += ring_buf[way, half, step - 2]

                @pl.when(step < 3)
                def _():
                    ring(way, half, step).start()

        @pl.when(group == 2)
        def _():
            finish(0)

    finish(1)

    for copy in stage_plane:
        copy.wait_recv()
    s_line[core * Z + z] = jnp.sum(s_plane[...], axis=0)
    for copy in stage_line:
        copy.start()

    lam = scaled_loadings(load_v[14, 1], stress_col, first_ref[path], rows)
    lh, ll = split(lam)
    cov = (dot_nt(lh, lh) + dot_nt(lh, ll) + dot_nt(ll, lh)) * (LN2 * LN2)
    r0 = start_ref[pl.ds(path, 1), :]

    for what in handed[0] + handed[1]:
        hand_over(*what).wait_recv()
    bar, total = unpack(out_buf[14, 1] + jnp.sum(z_buf[...], axis=0))
    out[0:NR, 0:NR] = stress_col * bar
    through = jnp.sum(jnp.where(rows >= cols, cov, 0.0) * total, axis=0, keepdims=True)
    direct = jnp.sum(jnp.where(eye, total, 0.0), axis=0, keepdims=True)
    out[80:81, 0:NR] = direct / r0 + through * (100.0 / ((100.0 + r0) * (100.0 + r0)))

    results = [
        pltpu.make_async_copy(out.at[part], out_hbm.at[part], out_sem.at[i])
        for i, part in enumerate((pl.ds(0, 88), pl.ds(88, 8)))
    ]
    results[0].start()

    for copy in stage_line:
        copy.wait_recv()
    out[88:96] = jnp.sum(s_line[...], axis=0)
    results[1].start()

    for half in range(2):
        for way in range(2):
            for step in range(3):
                ring(way, half, step).wait_send()
    for what in handed[0] + handed[1]:
        hand_over(*what).wait_send()
    for copy in stage_plane + stage_line:
        copy.wait_send()
    for copy in results:
        copy.wait()


def hand_on(packed, rate_out, vol_out, stress_out):
    rate_out[...] = packed[80:81, 0:NR]
    vol_out[0] = packed[0:NR, 0:NR]
    stress_out[...] = packed[88:89, 0:NR]


def body(start_rates, loadings, stress, increments, cotangent, first_active):
    log_paths = math.log2(WIDTH * X * Z)
    vmem = pl.BlockSpec(memory_space=pltpu.VMEM)
    anywhere = pl.BlockSpec(memory_space=pl.ANY)
    dma = pltpu.SemaphoreType.DMA
    summed = pl.pallas_call(
        lambda *refs: kernel(log_paths, *refs),
        out_shape=jax.ShapeDtypeStruct((96, 128), f32),
        in_specs=[anywhere] * 6,
        out_specs=anywhere,
        scratch_shapes=[
            pltpu.VMEM((1, NR), f32),
            pltpu.SMEM((2 * PAIRS,), jnp.int32),
            pltpu.VMEM((2 * PAIRS, NR), f32),
            pltpu.VMEM((96, 128), f32),
            pltpu.VMEM((PAIRS, 2, NR, NR), f32),
            pltpu.VMEM((PAIRS, 2, 2, NR, WIDTH), bf16),
            pltpu.VMEM((PAIRS, 2, NR, WIDTH), f32),
            pltpu.VMEM((PAIRS, 2, PACKED, 128), f32),
            pltpu.VMEM((2, 2, 3, 2, PACKED, 128), f32),
            pltpu.VMEM((Z - 1, PACKED, 128), f32),
            pltpu.VMEM((NR, NR), f32),
            pltpu.VMEM((SIXTEEN, 8, 128), f32),
            pltpu.VMEM((SIXTEEN, 8, 128), f32),
            dma((3,)),
            dma((2,)),
            dma((3, PAIRS, 2)),
            dma((2, 2, 3)),
            dma((2, 2, 3)),
            dma((Z - 1,)),
            dma((Z - 1,)),
            dma((2, SIXTEEN)),
            dma((2, SIXTEEN)),
        ],
        compiler_params=pltpu.CompilerParams(
            collective_id=0, has_side_effects=True, vmem_limit_bytes=56 * 2**20
        ),
        name="adjoint",
    )(
        stress[None],
        first_active,
        start_rates,
        loadings.reshape(X, Z, NR, NR),
        increments.reshape(X, Z, 2, NR, WIDTH),
        cotangent.reshape(X, Z, NR, WIDTH),
    )
    rate, vol, stress_gradient = pl.pallas_call(
        hand_on,
        out_shape=(
            jax.ShapeDtypeStruct((1, NR), f32),
            jax.ShapeDtypeStruct((1, NR, NR), f32),
            jax.ShapeDtypeStruct((1, NR), f32),
        ),
        in_specs=[vmem],
        out_specs=(vmem, vmem, vmem),
        name="results",
    )(summed)
    return rate, vol, stress_gradient[0]


def solution(mesh):
    return jax.shard_map(
        body,
        mesh=mesh,
        in_specs=(
            P("grp", None),
            P("grp", None, None),
            P(),
            P("grp", None, None, "path"),
            P("grp", None, "path"),
            P("grp"),
        ),
        out_specs=(P(("grp", "path"), None), P(("grp", "path"), None, None), P()),
        check_vma=False,
    )
```

time: 42.5 us -> 36.3 us (0.85)
  local copies, waits for them, and re-layouts: 3.66 us -> 0 us
  Pallas kernels: 38 us -> 35.5 us
    unnamed x3 -> x0, local copies, waits for them, and re-layouts: 3.66 us -> none
    pallas_call x1 -> x2, Pallas kernels: 38 us -> 35.5 us  [the longest x1 34.1 us: body(): pl.pallas_call(lambda *refs: kernel(log_paths, *refs), out_shape=jax.Shap...]
where the time goes in v2:
time: 36.3 us; the launch traced here: 36.2 us
  Pallas kernels  35.5 us (98%)
  between operations  0.64 us (2%)
    pallas_call x1, Pallas kernels, body(): pl.pallas_call(lambda *refs: kernel(log_paths, *refs), out_shape=jax.Shap...  34.1 us
    pallas_call x1, Pallas kernels, body(): pl.pallas_call(hand_on, out_shape=(jax.ShapeDtypeStruct((1, NR), f32), ja...  1.42 us

profile of v2, /device:TPU:1, one launch (start us, length us, event | category | flops | bytes accessed | tf_op | source)
XLA Modules:
  0.0 36.2 jit_solution(677080434255040196)
XLA Ops:
  0.6 34.1 %adjoint.1.packed = f32[96,128]{1,0:T(8,128)} custom-call(f32[1,80]{1,0:T(1,128)} %bitcast.8, s32[32]{0:T(128)} %refs_1_.1, f32[32,80]{1,0:T(8,128)} %refs_2_.1, f32[4,8,80,80]{3,2,1,0:T(8,128)} %bitcast.7, bf16[4,8,2,80,256]{4,3,2,1,0:T(8,128)(2,1)} %bitcast.5, f32[4,8,80,256]{3,2,1,0:T(8,128)} %bitcast.6), custom_call_target="tpu_custom_call" | custom-call | tf_op jit(solution)/shard_map/adjoint/pallas_call | solution.py:341
  34.7 1.4 %results.1 = (f32[1,80]{1,0:T(1,128)}, f32[1,80,80]{2,1,0:T(8,128)}, f32[1,80]{1,0:T(1,128)}) custom-call(f32[96,128]{1,0:T(8,128)} %adjoint.1.packed), custom_call_target="tpu_custom_call" | custom-call | tf_op jit(solution)/shard_map/results/pallas_call | solution.py:382

commit v3 on v2

--- a/solution.py
+++ b/solution.py
@@ -40,8 +40,13 @@
     return rows, cols
 
 
-def place(pair, k, x, z):
-    half, step, way = pair // 8, pair % 8 // 2, pair % 2
+STEPS = {(0, 0): 0, (0, 1): 1, (1, 0): 2, (0, 2): 3, (1, 1): 4, (0, 3): 5, (1, 2): 6, (1, 3): 7}
+
+
+def place(pair, k, x):
+    at, way = pair // 2, pair % 2
+    half = (at + 1) % 2 - (7 - at) // 7 + at // 7
+    step = (at + 1 - 2 * half) // 2
     reach = 2 - (step + 1) // 2
     side = lax.rem(step + way, 2)
     hops = 3 - 2 * half - side if k else 4 + 2 * half + side
@@ -49,64 +54,94 @@
 
 
 def scaled_loadings(load, stress_col, first, rows):
-    return jnp.where(rows >= first, load * stress_col, 0.0) * LOG2E
-
-
-def adjoint_of(items, stress_col, log_paths, emit):
+    return load * jnp.where(rows >= first, stress_col * LOG2E, 0.0)
+
+
+def forward(items, held, slot, masks, stress_col, log_paths):
     rows, cols = index_masks()
-    low, upp, eye = rows >= cols, rows <= cols, rows == cols
+    eye = rows == cols
+    for k, d in enumerate(items):
+        yield
+        d["lam"] = scaled_loadings(d["load"][...], stress_col, d["first"], rows)
+        d["lh"], d["ll"] = split(d["lam"])
+        held["lam"][slot, k] = d["lam"]
+    for d in items:
+        yield
+        d["cov"] = dot_nt(d["lh"], d["lh"])
+    for k, d in enumerate(items):
+        yield
+        drift = d["cov"] * masks[0]
+        r0 = d["r0"]
+        accrual = r0 / (100.0 + r0)
+        half = jnp.sum(d["lam"] * d["lam"], axis=1, keepdims=True) * (-0.5 * LN2)
+        c1 = jnp.sum(drift * accrual + jnp.where(eye, jnp.log2(r0), 0.0), axis=1, keepdims=True)
+        d["c1"] = half + c1 - math.log2(100.0)
+        d["c2"] = half + (math.log2(100.0) - log_paths)
+        d["left"] = jnp.concatenate([d["lh"], d["ll"], drift.astype(bf16)], axis=1)
+        held["back"][slot, k] = (d["cov"] * masks[1]).astype(bf16)
+    for d in items:
+        yield
+        z1 = d["z"][0]
+        d["e1"] = dot(d["left"][:, : 2 * NR], jnp.concatenate([z1, z1], axis=0))
+    for k, d in enumerate(items):
+        yield
+        mid = jnp.exp2(d["e1"] + d["c1"])
+        inverse = 1.0 / (1.0 + mid)
+        accrual = mid * inverse
+        d["mid"], d["a"] = mid, accrual.astype(bf16)
+        held["a"][slot, k] = d["a"]
+        held["slope"][slot, k] = accrual * inverse
+    for d in items:
+        yield
+        z2 = d["z"][1]
+        d["e2"] = dot(d["left"], jnp.concatenate([z2, z2, d["a"]], axis=0))
+    for k, d in enumerate(items):
+        yield
+        held["g2"][slot, k] = d["mid"] * jnp.exp2(d["e2"] + d["c2"]) * d["cot"][...]
+
+
+def adjoint(items, held, slot, emit):
+    rows, cols = index_masks()
+    low = rows >= cols
     ones = jnp.ones((16, WIDTH), bf16)
     gap = jnp.zeros((32, WIDTH), bf16)
-    for d in items:
-        d["lam"] = scaled_loadings(d["load"][...], stress_col, d["first"], rows)
-        d["lh"], d["ll"] = split(d["lam"])
-    for d in items:
-        d["cov"] = dot_nt(d["lh"], d["lh"])
-    for d in items:
-        drift = jnp.where(low, d["cov"], 0.0) * LN2
-        r0 = d["r0"]
-        d["a0"] = r0 / (100.0 + r0)
-        half = jnp.sum(d["lam"] * d["lam"], axis=1, keepdims=True) * (-0.5 * LN2)
-        d["c1"] = half + jnp.sum(drift * d["a0"] + jnp.where(eye, jnp.log2(r0), 0.0), axis=1, keepdims=True)
-        d["c2"] = half - log_paths
-        d["left"] = jnp.concatenate([d["lh"], d["ll"], drift.astype(bf16)], axis=1)
-        d["back"] = (jnp.where(upp, d["cov"], 0.0) * (LN2 * LN2)).astype(bf16)
-    for d in items:
-        z1 = d["z"][0]
-        d["e1"] = dot(d["left"][:, : 2 * NR], jnp.concatenate([z1, z1], axis=0))
-    for d in items:
-        mid = jnp.exp2(d["e1"] + d["c1"])
-        scaled = 0.01 * mid
-        inverse = 1.0 / (1.0 + scaled)
-        accrual = scaled * inverse
-        d["mid"], d["a"], d["slope"] = mid, accrual.astype(bf16), accrual * inverse
-    for d in items:
-        z2 = d["z"][1]
-        d["e2"] = dot(d["left"], jnp.concatenate([z2, z2, d["a"]], axis=0))
-    for d in items:
-        d["g2"] = d["mid"] * jnp.exp2(d["e2"] + d["c2"]) * d["cot"][...]
+    for k, d in enumerate(items):
+        yield
+        d["g2"] = held["g2"][slot, k]
         d["g2h"], d["g2l"] = split(d["g2"])
-    for d in items:
-        d["da"] = dot(d["back"], d["g2h"])
-    for d in items:
-        right = jnp.concatenate([d["z"][1], ones, gap, d["a"]], axis=0)
+    for k, d in enumerate(items):
+        yield
+        d["da"] = dot(held["back"][slot, k], d["g2h"])
+    for k, d in enumerate(items):
+        yield
+        right = jnp.concatenate([d["z"][1], ones, gap, held["a"][slot, k]], axis=0)
         d["sums2"] = dot_nt(jnp.concatenate([d["g2h"], d["g2l"]], axis=0), right)
-    for d in items:
-        g1h, g1l = split(d["g2"] + d["slope"] * d["da"])
+    for k, d in enumerate(items):
+        yield
+        g1h, g1l = split(d["g2"] + held["slope"][slot, k] * d["da"])
         right = jnp.concatenate([d["z"][0], ones], axis=0)
         d["sums1"] = dot_nt(jnp.concatenate([g1h, g1l], axis=0), right)
-    for d in items:
+    for k, d in enumerate(items):
+        yield
+        lam = held["lam"][slot, k]
+        lh, ll = split(lam)
         sum1 = d["sums1"][:NR] + d["sums1"][NR:]
         sum2 = d["sums2"][:NR, :128] + d["sums2"][NR:, :128]
         outer = d["sums2"][:NR, 128:208] + d["sums2"][NR:, 128:208]
         total1, total2 = sum1[:, NR : NR + 1], sum2[:, NR : NR + 1]
-        bar_cov = jnp.where(low, outer + total1 * d["a0"], 0.0)
+        bar_cov = jnp.where(low, outer + total1 * (d["r0"] / (100.0 + d["r0"])), 0.0)
         mh, ml = split((bar_cov + bar_cov.T) * LN2)
-        through = dot(
-            jnp.concatenate([mh, ml, mh], axis=1), jnp.concatenate([d["lh"], d["lh"], d["ll"]], axis=0)
-        )
-        bar = sum1[:, :NR] + sum2[:, :NR] + through - ((total1 + total2) * LN2) * d["lam"]
+        through = dot(jnp.concatenate([mh, ml, mh], axis=1), jnp.concatenate([lh, lh, ll], axis=0))
+        bar = sum1[:, :NR] + sum2[:, :NR] + through - ((total1 + total2) * LN2) * lam
         emit(d, jnp.where(rows >= d["first"], bar, 0.0), total1)
+
+
+def interleaved(*parts):
+    parts = list(parts)
+    while parts:
+        for part in list(parts):
+            if next(part, parts) is parts:
+                parts.remove(part)
 
 
 def pack(ref, bar, total):
@@ -132,6 +167,7 @@
     out_hbm,
     stress_ref, first_ref, start_ref, out,
     load_v, z_v, cot_v, out_buf, ring_buf, z_buf, acc, s_plane, s_line,
+    h_lam, h_back, h_a, h_slope, h_g2,
     small_sem, out_sem, in_sem, ring_send, ring_recv, z_send, z_recv, s_send, s_recv,
 ):
     g = lax.axis_index("grp")
@@ -139,7 +175,7 @@
     x, z = path // Z, lax.rem(path, Z)
 
     def owner(pair, k):
-        owner_x, hops = place(pair, k, x, z)
+        owner_x, hops = place(pair, k, x)
         return owner_x, lax.rem(z + hops, Z)
 
     def fetches(pair):
@@ -156,7 +192,7 @@
     for copy in small:
         copy.start()
 
-    @pl.loop(0, PAIRS)
+    @pl.loop(0, 4)
     def _(pair):
         for copy in fetches(pair):
             copy.start()
@@ -179,6 +215,11 @@
     for k in range(1, SIXTEEN):
         for peer in (plane_peer, line_peer):
             pl.semaphore_signal(barrier, inc=1, device_id=peer(k), device_id_type=MESH)
+
+    @pl.loop(4, PAIRS)
+    def _(pair):
+        for copy in fetches(pair):
+            copy.start()
 
     for copy in small:
         copy.wait()
@@ -189,7 +230,7 @@
 
     def ring(way, half, step):
         return pltpu.make_async_remote_copy(
-            src_ref=out_buf.at[8 * half + 2 * step + way],
+            src_ref=out_buf.at[2 * STEPS[half, step] + way],
             dst_ref=ring_buf.at[way, half, step],
             send_sem=ring_send.at[way, half, step],
             recv_sem=ring_recv.at[way, half, step],
@@ -200,7 +241,7 @@
     def hand_over(half, side, k):
         hops = 3 - 2 * half - side if k else 4 + 2 * half + side
         return pltpu.make_async_remote_copy(
-            src_ref=out_buf.at[8 * half + 7 - side, k],
+            src_ref=out_buf.at[2 * STEPS[half, 3] + 1 - side, k],
             dst_ref=z_buf.at[hops - 1],
             send_sem=z_send.at[hops - 1],
             recv_sem=z_recv.at[hops - 1],
@@ -213,7 +254,7 @@
     def finish(half):
         for way in range(2):
             ring(way, half, 2).wait_recv()
-            out_buf[8 * half + 7 - way] += ring_buf[way, half, 2]
+            out_buf[2 * STEPS[half, 3] + 1 - way] += ring_buf[way, half, 2]
         for what in handed[half]:
             hand_over(*what).start()
 
@@ -245,51 +286,70 @@
     stage_plane = share(s_plane, plane_peer, y * X + x, 0)
     stage_line = share(s_line, line_peer, core * Z + z, 1)
 
-    @pl.loop(0, 4)
-    def _(group):
+    masks = (jnp.where(rows >= cols, LN2, 0.0), jnp.where(rows <= cols, LN2 * LN2, 0.0))
+    held = dict(lam=h_lam, back=h_back, a=h_a, slope=h_slope, g2=h_g2)
+
+    def items(group):
+        return [scenario(4 * group + j, k) for j in range(4) for k in range(2)]
+
+    def start(group, slot):
         for j in range(4):
             for copy in fetches(4 * group + j):
                 copy.wait()
-        items = [scenario(4 * group + j, k) for j in range(4) for k in range(2)]
-        adjoint_of(items, stress_col, log_paths, emit)
-
-        @pl.when(group == 0)
+        return forward(items(group), held, slot, masks, stress_col, log_paths)
+
+    def send(half, step):
+        for way in range(2):
+            ring(way, half, step).start()
+
+    def take(half, step):
+        for way in range(2):
+            ring(way, half, step - 2).wait_recv()
+            out_buf[2 * STEPS[half, step] + way] += ring_buf[way, half, step - 2]
+
+    interleaved(start(0, 0))
+
+    @pl.loop(1, 4)
+    def _(group):
+        slot = lax.rem(group, 2)
+        ahead = start(group, slot)
+        interleaved(adjoint(items(group - 1), held, 1 - slot, emit), ahead)
+
+        @pl.when(group == 1)
         def _():
             pl.semaphore_wait(barrier, 2 * (SIXTEEN - 1))
+            send(0, 0)
+            send(0, 1)
+
+        @pl.when(group == 2)
+        def _():
+            send(1, 0)
 
         @pl.when(group == 3)
         def _():
-            part = jnp.sum(jnp.where(eye, jnp.sum(acc[...], axis=1, keepdims=True), 0.0), axis=0, keepdims=True)
-            s_plane[y * X + x, :, 0:NR] = jnp.broadcast_to(part, (8, NR))
-            s_plane[y * X + x, :, NR:128] = jnp.zeros((8, 128 - NR), f32)
-            for copy in stage_plane:
-                copy.start()
-
-        half = group // 2
-        for j in range(2):
-            step = 2 * (group % 2) + j
-            for way in range(2):
-
-                @pl.when(step >= 2)
-                def _():
-                    ring(way, half, step - 2).wait_recv()
-                    out_buf[8 * half + 2 * step + way] += ring_buf[way, half, step - 2]
-
-                @pl.when(step < 3)
-                def _():
-                    ring(way, half, step).start()
-
-        @pl.when(group == 2)
-        def _():
-            finish(0)
-
-    finish(1)
+            take(0, 2)
+            send(0, 2)
+            send(1, 1)
+
+    interleaved(adjoint(items(3), held, 1, emit))
+    part = jnp.sum(jnp.where(eye, jnp.sum(acc[...], axis=1, keepdims=True), 0.0), axis=0, keepdims=True)
+    s_plane[y * X + x, :, 0:NR] = jnp.broadcast_to(part, (8, NR))
+    s_plane[y * X + x, :, NR:128] = jnp.zeros((8, 128 - NR), f32)
+    for copy in stage_plane:
+        copy.start()
+    take(1, 2)
+    send(1, 2)
+    take(0, 3)
+    finish(0)
 
     for copy in stage_plane:
         copy.wait_recv()
     s_line[core * Z + z] = jnp.sum(s_plane[...], axis=0)
     for copy in stage_line:
         copy.start()
+
+    take(1, 3)
+    finish(1)
 
     lam = scaled_loadings(load_v[14, 1], stress_col, first_ref[path], rows)
     lh, ll = split(lam)
@@ -309,11 +369,6 @@
         for i, part in enumerate((pl.ds(0, 88), pl.ds(88, 8)))
     ]
     results[0].start()
-
-    for copy in stage_line:
-        copy.wait_recv()
-    out[88:96] = jnp.sum(s_line[...], axis=0)
-    results[1].start()
 
     for half in range(2):
         for way in range(2):
@@ -323,6 +378,11 @@
         hand_over(*what).wait_send()
     for copy in stage_plane + stage_line:
         copy.wait_send()
+    for copy in stage_line:
+        copy.wait_recv()
+    out[88:96] = jnp.sum(s_line[...], axis=0)
+    results[1].start()
+
     for copy in results:
         copy.wait()
 
@@ -357,6 +417,11 @@
             pltpu.VMEM((NR, NR), f32),
             pltpu.VMEM((SIXTEEN, 8, 128), f32),
             pltpu.VMEM((SIXTEEN, 8, 128), f32),
+            pltpu.VMEM((2, 8, NR, NR), f32),
+            pltpu.VMEM((2, 8, NR, NR), bf16),
+            pltpu.VMEM((2, 8, NR, WIDTH), bf16),
+            pltpu.VMEM((2, 8, NR, WIDTH), f32),
+            pltpu.VMEM((2, 8, NR, WIDTH), f32),
             dma((3,)),
             dma((2,)),
             dma((3, PAIRS, 2)),

time: 36.3 us -> 33.8 us (0.931)
  Pallas kernels: 35.5 us -> 33 us
    pallas_call x1, Pallas kernels: 34.1 us -> 31.5 us  [body(): pl.pallas_call(lambda *refs: kernel(log_paths, *refs), out_shape=jax.Shap...]
where the time goes in v3:
time: 33.8 us; the launch traced here: 33.6 us
  Pallas kernels  33 us (98%)
  between operations  0.64 us (2%)
    pallas_call x1, Pallas kernels, body(): pl.pallas_call(lambda *refs: kernel(log_paths, *refs), out_shape=jax.Shap...  31.5 us
    pallas_call x1, Pallas kernels, body(): pl.pallas_call(hand_on, out_shape=(jax.ShapeDtypeStruct((1, NR), f32), ja...  1.42 us

profile of v3, /device:TPU:1, one launch (start us, length us, event | category | flops | bytes accessed | tf_op | source)
XLA Modules:
  0.0 33.6 jit_solution(14003289786830764593)
XLA Ops:
  0.6 31.5 %adjoint.1.packed = f32[96,128]{1,0:T(8,128)} custom-call(f32[1,80]{1,0:T(1,128)} %bitcast.8, s32[32]{0:T(128)} %refs_1_.1, f32[32,80]{1,0:T(8,128)} %refs_2_.1, f32[4,8,80,80]{3,2,1,0:T(8,128)} %bitcast.7, bf16[4,8,2,80,256]{4,3,2,1,0:T(8,128)(2,1)} %bitcast.5, f32[4,8,80,256]{3,2,1,0:T(8,128)} %bitcast.6), custom_call_target="tpu_custom_call" | custom-call | tf_op jit(solution)/shard_map/adjoint/pallas_call | solution.py:401
  32.2 1.4 %results.1 = (f32[1,80]{1,0:T(1,128)}, f32[1,80,80]{2,1,0:T(8,128)}, f32[1,80]{1,0:T(1,128)}) custom-call(f32[96,128]{1,0:T(8,128)} %adjoint.1.packed), custom_call_target="tpu_custom_call" | custom-call | tf_op jit(solution)/shard_map/results/pallas_call | solution.py:447

commit v4 on v3

--- a/solution.py
+++ b/solution.py
@@ -144,6 +144,10 @@
                 parts.remove(part)
 
 
+def wait_for(ref, sem):
+    pltpu.make_async_copy(ref, ref, sem).wait()
+
+
 def pack(ref, bar, total):
     ref[:, 0:NR] = bar[:PACKED]
     ref[:, NR : NR + 1] = total[:PACKED]
@@ -180,7 +184,7 @@
 
     def fetches(pair):
         return [
-            pltpu.make_async_copy(hbm.at[owner(pair, k)], vmem.at[pair, k], in_sem.at[i, pair, k])
+            pltpu.make_async_copy(hbm.at[owner(pair, k)], vmem.at[pair, k], in_sem.at[i, pair // 4])
             for k in range(2)
             for i, (hbm, vmem) in enumerate(((load_hbm, load_v), (z_hbm, z_v), (cot_hbm, cot_v)))
         ]
@@ -231,9 +235,9 @@
     def ring(way, half, step):
         return pltpu.make_async_remote_copy(
             src_ref=out_buf.at[2 * STEPS[half, step] + way],
-            dst_ref=ring_buf.at[way, half, step],
-            send_sem=ring_send.at[way, half, step],
-            recv_sem=ring_recv.at[way, half, step],
+            dst_ref=ring_buf.at[half, step, way],
+            send_sem=ring_send,
+            recv_sem=ring_recv.at[half, step],
             device_id=x_peer(X - 1 if way else 1),
             device_id_type=MESH,
         )
@@ -243,18 +247,21 @@
         return pltpu.make_async_remote_copy(
             src_ref=out_buf.at[2 * STEPS[half, 3] + 1 - side, k],
             dst_ref=z_buf.at[hops - 1],
-            send_sem=z_send.at[hops - 1],
-            recv_sem=z_recv.at[hops - 1],
+            send_sem=z_send,
+            recv_sem=z_recv,
             device_id=z_peer(hops),
             device_id_type=MESH,
         )
 
     handed = [(0, side, k) for side in range(2) for k in range(2)], [(1, 0, 0), (1, 0, 1), (1, 1, 0)]
 
+    def arrived(half, step):
+        wait_for(ring_buf.at[half, step], ring_recv.at[half, step])
+
     def finish(half):
+        arrived(half, 2)
         for way in range(2):
-            ring(way, half, 2).wait_recv()
-            out_buf[2 * STEPS[half, 3] + 1 - way] += ring_buf[way, half, 2]
+            out_buf[2 * STEPS[half, 3] + 1 - way] += ring_buf[half, 2, way]
         for what in handed[half]:
             hand_over(*what).start()
 
@@ -275,8 +282,8 @@
             pltpu.make_async_remote_copy(
                 src_ref=buf.at[me],
                 dst_ref=buf.at[me],
-                send_sem=s_send.at[stage, k],
-                recv_sem=s_recv.at[stage, k],
+                send_sem=s_send.at[stage],
+                recv_sem=s_recv.at[stage],
                 device_id=peer(k),
                 device_id_type=MESH,
             )
@@ -293,9 +300,9 @@
         return [scenario(4 * group + j, k) for j in range(4) for k in range(2)]
 
     def start(group, slot):
-        for j in range(4):
-            for copy in fetches(4 * group + j):
-                copy.wait()
+        blocks = pl.ds(4 * group, 4)
+        for i, vmem in enumerate((load_v, z_v, cot_v)):
+            wait_for(vmem.at[blocks], in_sem.at[i, group])
         return forward(items(group), held, slot, masks, stress_col, log_paths)
 
     def send(half, step):
@@ -303,9 +310,9 @@
             ring(way, half, step).start()
 
     def take(half, step):
+        arrived(half, step - 2)
         for way in range(2):
-            ring(way, half, step - 2).wait_recv()
-            out_buf[2 * STEPS[half, step] + way] += ring_buf[way, half, step - 2]
+            out_buf[2 * STEPS[half, step] + way] += ring_buf[half, step - 2, way]
 
     interleaved(start(0, 0))
 
@@ -342,8 +349,7 @@
     take(0, 3)
     finish(0)
 
-    for copy in stage_plane:
-        copy.wait_recv()
+    wait_for(s_plane.at[pl.ds(0, SIXTEEN - 1)], s_recv.at[0])
     s_line[core * Z + z] = jnp.sum(s_plane[...], axis=0)
     for copy in stage_line:
         copy.start()
@@ -356,8 +362,7 @@
     cov = (dot_nt(lh, lh) + dot_nt(lh, ll) + dot_nt(ll, lh)) * (LN2 * LN2)
     r0 = start_ref[pl.ds(path, 1), :]
 
-    for what in handed[0] + handed[1]:
-        hand_over(*what).wait_recv()
+    wait_for(z_buf, z_recv)
     bar, total = unpack(out_buf[14, 1] + jnp.sum(z_buf[...], axis=0))
     out[0:NR, 0:NR] = stress_col * bar
     through = jnp.sum(jnp.where(rows >= cols, cov, 0.0) * total, axis=0, keepdims=True)
@@ -370,16 +375,11 @@
     ]
     results[0].start()
 
-    for half in range(2):
-        for way in range(2):
-            for step in range(3):
-                ring(way, half, step).wait_send()
-    for what in handed[0] + handed[1]:
-        hand_over(*what).wait_send()
-    for copy in stage_plane + stage_line:
-        copy.wait_send()
-    for copy in stage_line:
-        copy.wait_recv()
+    wait_for(out_buf.at[pl.ds(0, 12)], ring_send)
+    wait_for(z_buf, z_send)
+    for stage in range(2):
+        wait_for(s_line.at[pl.ds(0, SIXTEEN - 1)], s_send.at[stage])
+    wait_for(s_line.at[pl.ds(0, SIXTEEN - 1)], s_recv.at[1])
     out[88:96] = jnp.sum(s_line[...], axis=0)
     results[1].start()
 
@@ -412,7 +412,7 @@
             pltpu.VMEM((PAIRS, 2, 2, NR, WIDTH), bf16),
             pltpu.VMEM((PAIRS, 2, NR, WIDTH), f32),
             pltpu.VMEM((PAIRS, 2, PACKED, 128), f32),
-            pltpu.VMEM((2, 2, 3, 2, PACKED, 128), f32),
+            pltpu.VMEM((2, 3, 2, 2, PACKED, 128), f32),
             pltpu.VMEM((Z - 1, PACKED, 128), f32),
             pltpu.VMEM((NR, NR), f32),
             pltpu.VMEM((SIXTEEN, 8, 128), f32),
@@ -424,13 +424,13 @@
             pltpu.VMEM((2, 8, NR, WIDTH), f32),
             dma((3,)),
             dma((2,)),
-            dma((3, PAIRS, 2)),
-            dma((2, 2, 3)),
-            dma((2, 2, 3)),
-            dma((Z - 1,)),
-            dma((Z - 1,)),
-            dma((2, SIXTEEN)),
-            dma((2, SIXTEEN)),
+            dma((3, 4)),
+            dma(()),
+            dma((2, 3)),
+            dma(()),
+            dma(()),
+            dma((2,)),
+            dma((2,)),
         ],
         compiler_params=pltpu.CompilerParams(
             collective_id=0, has_side_effects=True, vmem_limit_bytes=56 * 2**20

time: 33.8 us -> 32 us (0.947)
  Pallas kernels: 33 us -> 31.2 us
    pallas_call x1, Pallas kernels: 31.5 us -> 29.8 us  [body(): pl.pallas_call(lambda *refs: kernel(log_paths, *refs), out_shape=jax.Shap...]
where the time goes in v4:
time: 32 us; the launch traced here: 31.9 us
  Pallas kernels  31.2 us (98%)
  between operations  0.64 us (2%)
    pallas_call x1, Pallas kernels, body(): pl.pallas_call(lambda *refs: kernel(log_paths, *refs), out_shape=jax.Shap...  29.8 us
    pallas_call x1, Pallas kernels, body(): pl.pallas_call(hand_on, out_shape=(jax.ShapeDtypeStruct((1, NR), f32), ja...  1.42 us

profile of v4, /device:TPU:1, one launch (start us, length us, event | category | flops | bytes accessed | tf_op | source)
XLA Modules:
  0.0 31.9 jit_solution(2176637572879399076)
XLA Ops:
  0.6 29.8 %adjoint.1.packed = f32[96,128]{1,0:T(8,128)} custom-call(f32[1,80]{1,0:T(1,128)} %bitcast.8, s32[32]{0:T(128)} %refs_1_.1, f32[32,80]{1,0:T(8,128)} %refs_2_.1, f32[4,8,80,80]{3,2,1,0:T(8,128)} %bitcast.7, bf16[4,8,2,80,256]{4,3,2,1,0:T(8,128)(2,1)} %bitcast.5, f32[4,8,80,256]{3,2,1,0:T(8,128)} %bitcast.6), custom_call_target="tpu_custom_call" | custom-call | tf_op jit(solution)/shard_map/adjoint/pallas_call | solution.py:401
  30.5 1.4 %results.1 = (f32[1,80]{1,0:T(1,128)}, f32[1,80,80]{2,1,0:T(8,128)}, f32[1,80]{1,0:T(1,128)}) custom-call(f32[96,128]{1,0:T(8,128)} %adjoint.1.packed), custom_call_target="tpu_custom_call" | custom-call | tf_op jit(solution)/shard_map/results/pallas_call | solution.py:447

commit v5 on v4

--- a/solution.py
+++ b/solution.py
@@ -131,7 +131,8 @@
         total1, total2 = sum1[:, NR : NR + 1], sum2[:, NR : NR + 1]
         bar_cov = jnp.where(low, outer + total1 * (d["r0"] / (100.0 + d["r0"])), 0.0)
         mh, ml = split((bar_cov + bar_cov.T) * LN2)
-        through = dot(jnp.concatenate([mh, ml, mh], axis=1), jnp.concatenate([lh, lh, ll], axis=0))
+        both = dot(jnp.concatenate([mh, ml], axis=0), lh)
+        through = both[:NR] + both[NR:] + dot(mh, ll)
         bar = sum1[:, :NR] + sum2[:, :NR] + through - ((total1 + total2) * LN2) * lam
         emit(d, jnp.where(rows >= d["first"], bar, 0.0), total1)
 
@@ -340,8 +341,7 @@
 
     interleaved(adjoint(items(3), held, 1, emit))
     part = jnp.sum(jnp.where(eye, jnp.sum(acc[...], axis=1, keepdims=True), 0.0), axis=0, keepdims=True)
-    s_plane[y * X + x, :, 0:NR] = jnp.broadcast_to(part, (8, NR))
-    s_plane[y * X + x, :, NR:128] = jnp.zeros((8, 128 - NR), f32)
+    s_plane[y * X + x] = jnp.concatenate([part, jnp.zeros((1, 128 - NR), f32)], axis=1)
     for copy in stage_plane:
         copy.start()
     take(1, 2)
@@ -380,7 +380,7 @@
     for stage in range(2):
         wait_for(s_line.at[pl.ds(0, SIXTEEN - 1)], s_send.at[stage])
     wait_for(s_line.at[pl.ds(0, SIXTEEN - 1)], s_recv.at[1])
-    out[88:96] = jnp.sum(s_line[...], axis=0)
+    out[88:89] = jnp.sum(s_line[...], axis=0)
     results[1].start()
 
     for copy in results:
@@ -415,8 +415,8 @@
             pltpu.VMEM((2, 3, 2, 2, PACKED, 128), f32),
             pltpu.VMEM((Z - 1, PACKED, 128), f32),
             pltpu.VMEM((NR, NR), f32),
-            pltpu.VMEM((SIXTEEN, 8, 128), f32),
-            pltpu.VMEM((SIXTEEN, 8, 128), f32),
+            pltpu.VMEM((SIXTEEN, 1, 128), f32),
+            pltpu.VMEM((SIXTEEN, 1, 128), f32),
             pltpu.VMEM((2, 8, NR, NR), f32),
             pltpu.VMEM((2, 8, NR, NR), bf16),
             pltpu.VMEM((2, 8, NR, WIDTH), bf16),

time: 32 us -> 30.7 us (0.959)
  Pallas kernels: 31.2 us -> 29.9 us
    pallas_call x1, Pallas kernels: 29.8 us -> 28.5 us  [body(): pl.pallas_call(lambda *refs: kernel(log_paths, *refs), out_shape=jax.Shap...]
where the time goes in v5:
time: 30.7 us; the launch traced here: 30.5 us
  Pallas kernels  29.9 us (97%)
  between operations  0.64 us (2%)
    pallas_call x1, Pallas kernels, body(): pl.pallas_call(lambda *refs: kernel(log_paths, *refs), out_shape=jax.Shap...  28.5 us
    pallas_call x1, Pallas kernels, body(): pl.pallas_call(hand_on, out_shape=(jax.ShapeDtypeStruct((1, NR), f32), ja...  1.42 us

profile of v5, /device:TPU:1, one launch (start us, length us, event | category | flops | bytes accessed | tf_op | source)
XLA Modules:
  0.0 30.5 jit_solution(7862096832251041019)
XLA Ops:
  0.6 28.5 %adjoint.1.packed = f32[96,128]{1,0:T(8,128)} custom-call(f32[1,80]{1,0:T(1,128)} %bitcast.8, s32[32]{0:T(128)} %refs_1_.1, f32[32,80]{1,0:T(8,128)} %refs_2_.1, f32[4,8,80,80]{3,2,1,0:T(8,128)} %bitcast.7, bf16[4,8,2,80,256]{4,3,2,1,0:T(8,128)(2,1)} %bitcast.5, f32[4,8,80,256]{3,2,1,0:T(8,128)} %bitcast.6), custom_call_target="tpu_custom_call" | custom-call | tf_op jit(solution)/shard_map/adjoint/pallas_call | solution.py:401
  29.1 1.4 %results.1 = (f32[1,80]{1,0:T(1,128)}, f32[1,80,80]{2,1,0:T(8,128)}, f32[1,80]{1,0:T(1,128)}) custom-call(f32[96,128]{1,0:T(8,128)} %adjoint.1.packed), custom_call_target="tpu_custom_call" | custom-call | tf_op jit(solution)/shard_map/results/pallas_call | solution.py:447

commit v6 on v5

--- a/solution.py
+++ b/solution.py
@@ -60,6 +60,8 @@
 def forward(items, held, slot, masks, stress_col, log_paths):
     rows, cols = index_masks()
     eye = rows == cols
+    pad = jnp.zeros((NR, 128 - NR), bf16)
+    gap = jnp.zeros((128 - NR, WIDTH), bf16)
     for k, d in enumerate(items):
         yield
         d["lam"] = scaled_loadings(d["load"][...], stress_col, d["first"], rows)
@@ -77,12 +79,13 @@
         c1 = jnp.sum(drift * accrual + jnp.where(eye, jnp.log2(r0), 0.0), axis=1, keepdims=True)
         d["c1"] = half + c1 - math.log2(100.0)
         d["c2"] = half + (math.log2(100.0) - log_paths)
-        d["left"] = jnp.concatenate([d["lh"], d["ll"], drift.astype(bf16)], axis=1)
+        d["left"] = jnp.concatenate([d["lh"], pad, d["ll"]], axis=1)
+        d["drift"] = drift.astype(bf16)
         held["back"][slot, k] = (d["cov"] * masks[1]).astype(bf16)
     for d in items:
         yield
         z1 = d["z"][0]
-        d["e1"] = dot(d["left"][:, : 2 * NR], jnp.concatenate([z1, z1], axis=0))
+        d["e1"] = dot(d["left"], jnp.concatenate([z1, gap, z1], axis=0))
     for k, d in enumerate(items):
         yield
         mid = jnp.exp2(d["e1"] + d["c1"])
@@ -94,7 +97,7 @@
     for d in items:
         yield
         z2 = d["z"][1]
-        d["e2"] = dot(d["left"], jnp.concatenate([z2, z2, d["a"]], axis=0))
+        d["e2"] = dot(d["left"], jnp.concatenate([z2, gap, z2], axis=0)) + dot(d["drift"], d["a"])
     for k, d in enumerate(items):
         yield
         held["g2"][slot, k] = d["mid"] * jnp.exp2(d["e2"] + d["c2"]) * d["cot"][...]
@@ -104,6 +107,7 @@
     rows, cols = index_masks()
     low = rows >= cols
     ones = jnp.ones((16, WIDTH), bf16)
+    many = jnp.ones((128, WIDTH), bf16)
     gap = jnp.zeros((32, WIDTH), bf16)
     for k, d in enumerate(items):
         yield
@@ -119,21 +123,22 @@
     for k, d in enumerate(items):
         yield
         g1h, g1l = split(d["g2"] + held["slope"][slot, k] * d["da"])
-        right = jnp.concatenate([d["z"][0], ones], axis=0)
+        right = jnp.concatenate([d["z"][0], many], axis=0)
         d["sums1"] = dot_nt(jnp.concatenate([g1h, g1l], axis=0), right)
     for k, d in enumerate(items):
         yield
         lam = held["lam"][slot, k]
         lh, ll = split(lam)
-        sum1 = d["sums1"][:NR] + d["sums1"][NR:]
+        sum1 = d["sums1"][:NR, :128] + d["sums1"][NR:, :128]
+        whole1 = d["sums1"][:NR, 128:208] + d["sums1"][NR:, 128:208]
         sum2 = d["sums2"][:NR, :128] + d["sums2"][NR:, :128]
         outer = d["sums2"][:NR, 128:208] + d["sums2"][NR:, 128:208]
         total1, total2 = sum1[:, NR : NR + 1], sum2[:, NR : NR + 1]
-        bar_cov = jnp.where(low, outer + total1 * (d["r0"] / (100.0 + d["r0"])), 0.0)
+        bar_cov = jnp.where(low, outer + whole1 * (d["r0"] / (100.0 + d["r0"])), 0.0)
         mh, ml = split((bar_cov + bar_cov.T) * LN2)
         both = dot(jnp.concatenate([mh, ml], axis=0), lh)
         through = both[:NR] + both[NR:] + dot(mh, ll)
-        bar = sum1[:, :NR] + sum2[:, :NR] + through - ((total1 + total2) * LN2) * lam
+        bar = sum1[:, :NR] + sum2[:, :NR] + through - ((whole1 + total2) * LN2) * lam
         emit(d, jnp.where(rows >= d["first"], bar, 0.0), total1)
 
 

time: 30.7 us -> 30 us (0.977)
  Pallas kernels: 29.9 us -> 29.2 us
    pallas_call x1, Pallas kernels: 28.5 us -> 27.8 us  [body(): pl.pallas_call(lambda *refs: kernel(log_paths, *refs), out_shape=jax.Shap...]
where the time goes in v6:
time: 30 us; the launch traced here: 29.8 us
  Pallas kernels  29.2 us (97%)
  between operations  0.64 us (2%)
    pallas_call x1, Pallas kernels, body(): pl.pallas_call(lambda *refs: kernel(log_paths, *refs), out_shape=jax.Shap...  27.8 us
    pallas_call x1, Pallas kernels, body(): pl.pallas_call(hand_on, out_shape=(jax.ShapeDtypeStruct((1, NR), f32), ja...  1.42 us

profile of v6, /device:TPU:1, one launch (start us, length us, event | category | flops | bytes accessed | tf_op | source)
XLA Modules:
  0.0 29.8 jit_solution(5359184995642557324)
XLA Ops:
  0.6 27.8 %adjoint.1.packed = f32[96,128]{1,0:T(8,128)} custom-call(f32[1,80]{1,0:T(1,128)} %bitcast.8, s32[32]{0:T(128)} %refs_1_.1, f32[32,80]{1,0:T(8,128)} %refs_2_.1, f32[4,8,80,80]{3,2,1,0:T(8,128)} %bitcast.7, bf16[4,8,2,80,256]{4,3,2,1,0:T(8,128)(2,1)} %bitcast.5, f32[4,8,80,256]{3,2,1,0:T(8,128)} %bitcast.6), custom_call_target="tpu_custom_call" | custom-call | tf_op jit(solution)/shard_map/adjoint/pallas_call | solution.py:406
  28.4 1.4 %results.1 = (f32[1,80]{1,0:T(1,128)}, f32[1,80,80]{2,1,0:T(8,128)}, f32[1,80]{1,0:T(1,128)}) custom-call(f32[96,128]{1,0:T(8,128)} %adjoint.1.packed), custom_call_target="tpu_custom_call" | custom-call | tf_op jit(solution)/shard_map/results/pallas_call | solution.py:452

commit v7 on v6

--- a/solution.py
+++ b/solution.py
@@ -342,7 +342,6 @@
         def _():
             take(0, 2)
             send(0, 2)
-            send(1, 1)
 
     interleaved(adjoint(items(3), held, 1, emit))
     part = jnp.sum(jnp.where(eye, jnp.sum(acc[...], axis=1, keepdims=True), 0.0), axis=0, keepdims=True)
@@ -351,6 +350,7 @@
         copy.start()
     take(1, 2)
     send(1, 2)
+    send(1, 1)
     take(0, 3)
     finish(0)
 

time: 30 us -> 29.4 us (0.980)
  Pallas kernels: 29.2 us -> 28.6 us
    pallas_call x1, Pallas kernels: 27.8 us -> 27.1 us  [body(): pl.pallas_call(lambda *refs: kernel(log_paths, *refs), out_shape=jax.Shap...]
where the time goes in v7:
time: 29.4 us; the launch traced here: 29.2 us
  Pallas kernels  28.6 us (97%)
  between operations  0.64 us (2%)
    pallas_call x1, Pallas kernels, body(): pl.pallas_call(lambda *refs: kernel(log_paths, *refs), out_shape=jax.Shap...  27.1 us
    pallas_call x1, Pallas kernels, body(): pl.pallas_call(hand_on, out_shape=(jax.ShapeDtypeStruct((1, NR), f32), ja...  1.42 us

profile of v7, /device:TPU:1, one launch (start us, length us, event | category | flops | bytes accessed | tf_op | source)
XLA Modules:
  0.0 29.2 jit_solution(13887732590609884328)
XLA Ops:
  0.6 27.1 %adjoint.1.packed = f32[96,128]{1,0:T(8,128)} custom-call(f32[1,80]{1,0:T(1,128)} %bitcast.8, s32[32]{0:T(128)} %refs_1_.1, f32[32,80]{1,0:T(8,128)} %refs_2_.1, f32[4,8,80,80]{3,2,1,0:T(8,128)} %bitcast.7, bf16[4,8,2,80,256]{4,3,2,1,0:T(8,128)(2,1)} %bitcast.5, f32[4,8,80,256]{3,2,1,0:T(8,128)} %bitcast.6), custom_call_target="tpu_custom_call" | custom-call | tf_op jit(solution)/shard_map/adjoint/pallas_call | solution.py:406
  27.8 1.4 %results.1 = (f32[1,80]{1,0:T(1,128)}, f32[1,80,80]{2,1,0:T(8,128)}, f32[1,80]{1,0:T(1,128)}) custom-call(f32[96,128]{1,0:T(8,128)} %adjoint.1.packed), custom_call_target="tpu_custom_call" | custom-call | tf_op jit(solution)/shard_map/results/pallas_call | solution.py:452

commit v8 on v7

--- a/solution.py
+++ b/solution.py
@@ -133,13 +133,13 @@
         whole1 = d["sums1"][:NR, 128:208] + d["sums1"][NR:, 128:208]
         sum2 = d["sums2"][:NR, :128] + d["sums2"][NR:, :128]
         outer = d["sums2"][:NR, 128:208] + d["sums2"][NR:, 128:208]
-        total1, total2 = sum1[:, NR : NR + 1], sum2[:, NR : NR + 1]
+        total2 = sum2[:, NR : NR + 1]
         bar_cov = jnp.where(low, outer + whole1 * (d["r0"] / (100.0 + d["r0"])), 0.0)
         mh, ml = split((bar_cov + bar_cov.T) * LN2)
         both = dot(jnp.concatenate([mh, ml], axis=0), lh)
         through = both[:NR] + both[NR:] + dot(mh, ll)
         bar = sum1[:, :NR] + sum2[:, :NR] + through - ((whole1 + total2) * LN2) * lam
-        emit(d, jnp.where(rows >= d["first"], bar, 0.0), total1)
+        emit(d, jnp.where(rows >= d["first"], bar, 0.0), sum1)
 
 
 def interleaved(*parts):
@@ -154,14 +154,12 @@
     pltpu.make_async_copy(ref, ref, sem).wait()
 
 
-def pack(ref, bar, total):
+def pack(ref, bar, spread):
     ref[:, 0:NR] = bar[:PACKED]
-    ref[:, NR : NR + 1] = total[:PACKED]
-    rest = jnp.concatenate([bar[PACKED:], total[PACKED:]], axis=1)
-    ref[0:24, 81:128] = rest[:, 0:47]
-    ref[24:48, 81:115] = rest[:, 47:81]
-    ref[24:48, 115:128] = jnp.zeros((24, 13), f32)
-    ref[48:56, 81:128] = jnp.zeros((8, 47), f32)
+    ref[:, NR:128] = spread[:PACKED, NR:128]
+    ref[0:24, 81:128] = bar[PACKED:, 0:47]
+    ref[24:48, 81:114] = bar[PACKED:, 47:NR]
+    ref[24:48, 114:115] = spread[PACKED:, 114:115]
 
 
 def unpack(value):
@@ -271,8 +269,8 @@
         for what in handed[half]:
             hand_over(*what).start()
 
-    def emit(d, bar, total):
-        pack(d["out"], bar, total)
+    def emit(d, bar, spread):
+        pack(d["out"], bar, spread)
         acc[...] += d["load"][...] * bar
 
     def scenario(pair, k):

time: 29.4 us -> 29.3 us (level)
  no operation moved by 1% of the time
where the time goes in v8:
time: 29.3 us; the launch traced here: 29.2 us
  Pallas kernels  28.5 us (97%)
  between operations  0.64 us (2%)
    pallas_call x1, Pallas kernels, body(): pl.pallas_call(lambda *refs: kernel(log_paths, *refs), out_shape=jax.Shap...  27.1 us
    pallas_call x1, Pallas kernels, body(): pl.pallas_call(hand_on, out_shape=(jax.ShapeDtypeStruct((1, NR), f32), ja...  1.42 us

profile of v8, /device:TPU:1, one launch (start us, length us, event | category | flops | bytes accessed | tf_op | source)
XLA Modules:
  0.0 29.2 jit_solution(4505581722485849553)
XLA Ops:
  0.6 27.1 %adjoint.1.packed = f32[96,128]{1,0:T(8,128)} custom-call(f32[1,80]{1,0:T(1,128)} %bitcast.8, s32[32]{0:T(128)} %refs_1_.1, f32[32,80]{1,0:T(8,128)} %refs_2_.1, f32[4,8,80,80]{3,2,1,0:T(8,128)} %bitcast.7, bf16[4,8,2,80,256]{4,3,2,1,0:T(8,128)(2,1)} %bitcast.5, f32[4,8,80,256]{3,2,1,0:T(8,128)} %bitcast.6), custom_call_target="tpu_custom_call" | custom-call | tf_op jit(solution)/shard_map/adjoint/pallas_call | solution.py:404
  27.8 1.4 %results.1 = (f32[1,80]{1,0:T(1,128)}, f32[1,80,80]{2,1,0:T(8,128)}, f32[1,80]{1,0:T(1,128)}) custom-call(f32[96,128]{1,0:T(8,128)} %adjoint.1.packed), custom_call_target="tpu_custom_call" | custom-call | tf_op jit(solution)/shard_map/results/pallas_call | solution.py:450
